TPU v7x, 512 devices: a whole 4x8x8 slice. The times are simulated.
512 devices in a mesh: passage: 32 (over x, y), sub: 16 (over z, core).
Axes of the slice: x: 4, y: 8, z: 8, core: 2. Of those that a mesh axis runs over, the one named last changes fastest.
Arguments:
- block_vectors: float32 [32, 131072], P(None, ('passage', 'sub')), may hold values from -75 to 75
- stiffness: float32 [131072], P(('passage', 'sub')), may hold values from 2 to 8
- mass_diag: float32 [131072], P(('passage', 'sub')), may hold values from 0.5 to 2
- kblocks: float32 [1024, 4, 128, 128], P(('passage', 'sub')), may hold values from -0.25 to 0.25
- block_cols: int32 [1024, 4], P(('passage', 'sub')), may hold values from 0 to 5
- slot_node: int32 [524288], P(('passage', 'sub')), may hold values from 0 to 255
- slot_owner: int32 [524288, 1], P(('passage', 'sub')), may hold values from 0 to 15; in each aligned block of 1024 rows (0 to 1023, 1024 to 2047, ...) at most 128 rows name the same one
- slot_cell: int32 [524288], P(('passage', 'sub')), may hold values from 0 to 8191
- slot_weight: float32 [524288], P(('passage', 'sub')), may hold values from 0.5 to 4
- live_slots: int32 [512], P(('passage', 'sub')), may hold values from 768 to 1024, as said below
Outputs:
- residual: float32 [32, 131072], P(None, ('passage', 'sub'))
- gram_stiff: float32 [64, 64], replicated
- gram_plain: float32 [64, 64], replicated
Inputs may be any that keep to these rules, and one draw needn't show every extreme that they name: `slot_owner`: per device at most 128 slots name the same owner, and some device reaches 128 for some owner. `live_slots`: some device has all 1024 slots live.
All inputs are finite; a program needn't handle non-finite values.
Results may differ from a plain program's by a relative error of at most 0.00019.
Values sent between devices are 32-bit elements; how exact they have to be, the bound alone decides.
A program may use at most 64 MiB of HBM per device.

v0:
```python
import jax
import jax.numpy as jnp
from jax import lax
from jax.sharding import PartitionSpec as P

CX = 8
CY = 8
CZ = 128
center_weight = 15.0
lower_bound = 1.0 / 15.0
upper_bound = 17.0 / 15.0
middle = (upper_bound + lower_bound) / 2.0
radius = (upper_bound - lower_bound) / 2.0
sigma_ratio = middle / radius
first_rho = 1.0 / sigma_ratio
second_rho = 1.0 / (2.0 * sigma_ratio - first_rho)
third_rho = 1.0 / (2.0 * sigma_ratio - second_rho)


def padded_2(block, sides, width, periodic):
    for axis, dim in sides:
        count = lax.axis_size(axis)
        forward = [(i, i + 1) for i in range(count - 1)]
        if periodic:
            forward.append((count - 1, 0))
        backward = [(target, source) for source, target in forward]
        low = lax.ppermute(
            lax.slice_in_dim(block, block.shape[dim] - width, None, axis=dim), axis, forward
        )
        high = lax.ppermute(lax.slice_in_dim(block, 0, width, axis=dim), axis, backward)
        block = jnp.concatenate([low, block, high], axis=dim)
    return block


def laplace_inner(padded):
    rows_one = padded.shape[1] - 2
    rows_two = padded.shape[2] - 2
    depth = padded.shape[3]
    zpadded = jnp.pad(padded, ((0, 0), (0, 0), (0, 0), (1, 1)))
    neighbours = jnp.zeros((padded.shape[0], rows_one, rows_two, depth), jnp.float32)
    for offset_one in range(3):
        for offset_two in range(3):
            for offset_three in range(3):
                distance = abs(offset_one - 1) + abs(offset_two - 1) + abs(offset_three - 1)
                if distance == 0:
                    continue
                weight = 0.5 ** (distance - 1)
                neighbours = (
                    neighbours
                    + weight
                    * zpadded[
                        :,
                        offset_one : offset_one + rows_one,
                        offset_two : offset_two + rows_two,
                        offset_three : offset_three + depth,
                    ]
                )
    return center_weight * padded[:, 1:-1, 1:-1, :] - neighbours


def extend_field(field):
    wider = padded_2(field, (("passage", 1),), 1, True)
    return padded_2(wider, (("sub", 2),), 1, False)


def pressure_solve(source):
    first = source / (center_weight * middle)
    resid = source - laplace_inner(extend_field(first))
    second_step = second_rho * first_rho * first + 2.0 * second_rho / radius * (
        resid / center_weight
    )
    second = first + second_step
    resid = source - laplace_inner(extend_field(second))
    third_step = third_rho * second_rho * second_step + 2.0 * third_rho / radius * (
        resid / center_weight
    )
    result = second + third_step
    return result


def stiffness_apply(field, block_cols, kblocks, stiffness):
    width, local = field.shape
    block_size = kblocks.shape[2]
    window = padded_2(field, (("sub", 1),), local, False)
    blocks = window.reshape(width, 3 * local // block_size, block_size)
    gathered = blocks[:, block_cols]
    mixed = jnp.einsum("mrnb,rnbk->mrk", gathered, kblocks, precision=lax.Precision.HIGHEST)
    return stiffness[None, :] * field + mixed.reshape(width, local)


def inner(left, right):
    return lax.dot_general(
        left,
        right,
        (((1,), (1,)), ((), ())),
        precision=lax.Precision.HIGHEST,
        preferred_element_type=jnp.float32,
    )


def body(
    block_vectors,
    stiffness,
    mass_diag,
    kblocks,
    block_cols,
    slot_node,
    slot_owner,
    slot_cell,
    slot_weight,
    live_slots,
):
    modes, local = block_vectors.shape
    groups = lax.axis_size("sub")
    slots = slot_node.shape[0]
    capacity = 2 * slots // groups
    total = local * lax.axis_size("passage") * groups
    live = (jnp.arange(slots, dtype=jnp.int32) < live_slots[0]).astype(jnp.float32)
    scaled = slot_weight * live
    owner = slot_owner[:, 0]
    onehot = (owner[:, None] == jnp.arange(groups, dtype=jnp.int32)[None, :]).astype(jnp.int32)
    before = jnp.cumsum(onehot, axis=0) - onehot
    target = owner * capacity + jnp.sum(before * onehot, axis=1)
    cells_out = (
        jnp.zeros((groups * capacity,), jnp.int32)
        .at[target]
        .set(slot_cell)
        .reshape(groups, capacity)
    )
    cells_in = lax.all_to_all(cells_out, "sub", split_axis=0, concat_axis=0, tiled=True).reshape(-1)
    stiff_image = stiffness_apply(block_vectors, block_cols, kblocks, stiffness)
    values = block_vectors[:, slot_node] * scaled[None, :]
    outgoing = (
        jnp.zeros((modes, groups * capacity), jnp.float32)
        .at[:, target]
        .set(values)
        .reshape(modes, groups, capacity)
    )
    incoming = lax.all_to_all(outgoing, "sub", split_axis=1, concat_axis=1, tiled=True).reshape(
        modes, -1
    )
    source = (
        jnp.zeros((modes, CX * CY * CZ), jnp.float32)
        .at[:, cells_in]
        .add(incoming)
        .reshape(modes, CX, CY, CZ)
    )
    press = pressure_solve(source).reshape(modes, -1)
    picked = press[:, cells_in].reshape(modes, groups, capacity)
    returned = lax.all_to_all(picked, "sub", split_axis=1, concat_axis=1, tiled=True).reshape(
        modes, -1
    )
    forces = returned[:, target] * scaled[None, :]
    mass_image = mass_diag[None, :] * block_vectors + jnp.zeros((modes, local), jnp.float32).at[
        :, slot_node
    ].add(forces)
    numer, denom = lax.psum(
        (jnp.sum(block_vectors * stiff_image, axis=1), jnp.sum(block_vectors * mass_image, axis=1)),
        ("passage", "sub"),
    )
    theta = numer / denom
    residual = stiff_image - theta[:, None] * mass_image
    stiff_resid = stiffness_apply(residual, block_cols, kblocks, stiffness)
    search = jnp.concatenate([block_vectors, residual], axis=0)
    image = jnp.concatenate([stiff_image, stiff_resid], axis=0)
    gram_stiff, gram_plain = lax.psum(
        (inner(search, image), inner(search, search)), ("passage", "sub")
    )
    return (residual, gram_stiff / total, gram_plain / total)


def solution(mesh):
    return jax.shard_map(
        body,
        mesh=mesh,
        in_specs=(
            P(None, ("passage", "sub")),
            P(("passage", "sub")),
            P(("passage", "sub")),
            P(("passage", "sub"), None, None, None),
            P(("passage", "sub"), None),
            P(("passage", "sub")),
            P(("passage", "sub"), None),
            P(("passage", "sub")),
            P(("passage", "sub")),
            P(("passage", "sub")),
        ),
        out_specs=(P(None, ("passage", "sub")), P(), P()),
        check_vma=False,
    )
```

profile of v0, /device:TPU:1, one launch (start us, length us, event | category | flops | bytes accessed | tf_op | source)
XLA Modules:
  0.0 407.7 jit_solution(4970201615528179702)
XLA Ops:
  1.4 4.5 %reduce-window.6 = s32[16,8,128]{2,1,0:T(8,128)S(1)} reduce-window(s32[16,8,128]{2,1,0:T(8,128)S(1)} %fusion.68, s32[]{:T(128)} %constant.17.clone.1), window={size=1x1x128 pad=0_0x0_0x127_0}, to_apply=%region_2.3 | reduce-window | flops 2080768 | bytes 131076 | tf_op jit(solution)/shard_map/reduce-window
  7.7 5.0 %scatter_custom_fusion = s32[2048]{0:T(1024)} fusion(s32[1024]{0:T(1024)S(1)} %bitcast.91, s32[1024]{0:T(1024)} %param.17, s32[]{:T(128)} %constant.17.clone.1), kind=kCustom, calls=%fused_computation.178 | custom fusion | bytes 8704 | tf_op jit(solution)/shard_map/scatter | solution.py:127
  12.8 11.8 %all-to-all-start = ((s32[16,1,128]{2,1,0:T(1,128)}), s32[16,1,128]{2,1,0:T(1,128)S(1)}, u32[]{:S(2)}, u32[]{:S(2)}) async-start(s32[16,1,128]{2,1,0:T(1,128)} %bitcast.12), calls=%async_computation | async-start | bytes 16384 | tf_op jit(solution)/shard_map/all_to_all | solution.py:130
  28.1 6.6 %scatter_custom_fusion.1 = f32[32,2048]{0,1:T(8,128)S(1)} fusion(s32[1024]{0:T(1024)S(1)} %bitcast.92, f32[]{:T(128)} %constant.19.clone.1, f32[1024]{0:T(1024)S(1)} %fusion.72, f32[32,256]{0,1:T(8,128)S(1)} %copy.184, s32[1024]{0:T(1024)S(1)} %get-tuple-element.42), kind=kCustom, calls=%fused_computation.133 | custom fusion | flops 32768 | bytes 401412 | tf_op jit(solution)/shard_map/scatter | solution.py:136
  35.7 7.2 %all-to-all-start.1 = ((f32[32,16,128]{2,0,1:T(8,128)}), f32[32,16,128]{2,0,1:T(8,128)S(1)}, u32[]{:S(2)}, u32[]{:S(2)}) async-start(f32[32,16,128]{2,0,1:T(8,128)} %copy.192), calls=%async_computation.1 | async-start | bytes 524288 | tf_op jit(solution)/shard_map/all_to_all | solution.py:139
  42.9 11.7 %all-to-all-done.1 = f32[32,16,128]{2,0,1:T(8,128)S(1)} async-done(((f32[32,16,128]{2,0,1:T(8,128)}), f32[32,16,128]{2,0,1:T(8,128)S(1)}, u32[]{:S(2)}, u32[]{:S(2)}) %all-to-all-start.1) | async-done | bytes 262176 | tf_op jit(solution)/shard_map/all_to_all | solution.py:139
  55.0 15.8 %scatter_custom_fusion.2 = f32[32,8192]{0,1:T(8,128)} fusion(s32[2048]{0:T(1024)S(1)} %bitcast.87, f32[2048,32]{1,0:T(8,128)S(1)} %copy.194, f32[]{:T(128)} %constant.19.clone.1), kind=kCustom, calls=%fused_computation.24 | custom fusion | flops 65536 | bytes 1048580 | tf_op jit(solution)/shard_map/scatter-add | solution.py:145
  77.2 6.0 %collective-permute-start.3 = (f32[32,1,8,128]{3,2,1,0:T(8,128)S(1)}, f32[32,1,8,128]{3,2,1,0:T(8,128)S(1)}, u32[]{:S(2)}, u32[]{:S(2)}) collective-permute-start(f32[32,1,8,128]{3,2,1,0:T(8,128)S(1)} %get-tuple-element.41), channel_id=1, source_target_pairs={{16,0},{32,16},{48,32},{64,48},{80,64},{96,80},{112,96},{128,112},... | collective-permute-start | bytes 393224 | tf_op jit(solution)/shard_map/ppermute | solution.py:30
  101.8 5.4 %select_maximum_fusion.4 = f32[32,10,10,130]{3,2,1,0:T(8,128)} fusion(f32[32,10,1,128]{3,2,1,0:T(1,128)S(1)} %copy.201, f32[32,10,1,128]{3,2,1,0:T(1,128)S(1)} %copy.200, f32[32,1,8,128]{3,2,1,0:T(8,128)S(1)} %collective-permute-done.3, f32[32,8,8,128]{3,2,1,0:T(8,128)S(1)} %broadcast_multiply_fusion, f32[32,1,8,128]{3,2,1,0:T(8,128)S(1)} %collective-permute-done.2), kind=kLoop, calls=%fused_computation.15 | loop fusion | flops 4992000 | bytes 3302400 | tf_op jit(solution)/shard_map/concatenate | solution.py:31
  107.2 23.2 %fusion.77 = (f32[32,8,8,128]{3,2,1,0:T(8,128)S(1)}, f32[32,8,8,128]{3,2,1,0:T(8,128)}) fusion(f32[32,8,8,128]{3,2,1,0:T(8,128)} %copy-done.1, f32[32,10,10,130]{3,2,1,0:T(8,128)} %select_maximum_fusion.4, f32[32,10,9,128]{3,2,1,0:T(8,128)} %get-tuple-element.35, f32[32,1,8,128]{3,2,1,0:T(8,128)S(1)} %collective-permute-done.3, ...), kind=kLoop, calls=%fused_computation.188 | loop fusion | flops 14417920 | bytes 29622272 | tf_op jit(solution)/shard_map/add | solution.py:72
  132.3 6.7 %collective-permute-start.7 = (f32[32,1,8,128]{3,2,1,0:T(8,128)S(1)}, f32[32,1,8,128]{3,2,1,0:T(8,128)S(1)}, u32[]{:S(2)}, u32[]{:S(2)}) collective-permute-start(f32[32,1,8,128]{3,2,1,0:T(8,128)S(1)} %get-tuple-element.39), channel_id=1, source_target_pairs={{16,0},{32,16},{48,32},{64,48},{80,64},{96,80},{112,96},{128,112},... | collective-permute-start | bytes 393224 | tf_op jit(solution)/shard_map/ppermute | solution.py:30
  141.1 4.0 collective-permute-start.8
  147.5 4.2 %collective-permute-done.9 = f32[32,10,1,128]{3,0,2,1:T(8,128)S(1)} collective-permute-done((f32[32,10,1,128]{3,0,2,1:T(8,128)S(1)}, f32[32,10,1,128]{3,0,2,1:T(8,128)S(1)}, u32[]{:S(2)}, u32[]{:S(2)}) %collective-permute-start.9) | collective-permute-done | bytes 163872 | tf_op jit(solution)/shard_map/ppermute | solution.py:30
  154.2 3.9 select_maximum_fusion
  158.1 6.5 %fusion.8 = f32[32,8,8,128]{3,2,1,0:T(8,128)} fusion(f32[32,8,8,128]{3,2,1,0:T(8,128)S(1)} %get-tuple-element.28, f32[32,8,8,128]{3,2,1,0:T(8,128)S(1)} %copy-done.2, f32[32,10,10,130]{3,2,1,0:T(8,128)S(1)} %select_maximum_fusion, f32[32,10,9,128]{3,2,1,0:T(8,128)} %get-tuple-element.31, f32[32,1,8,128]{3,2,1,0:T(8,128)S(1)} %collective-permute-done.7, ...), kind=kLoop, calls=%fused_computation.34 | loop fusion | flops 14155776 | bytes 29622272 | tf_op jit(solution)/shard_map/add | solution.py:77
  164.6 3.6 copy.212
  168.2 7.7 %gather_fusion.1 = f32[2048,32]{1,0:T(8,128)S(1)} fusion(f32[32,8192]{0,1:T(8,128)} %bitcast.78, s32[2048]{0:T(1024)S(1)} %broadcast_clamp_fusion), kind=kCustom, calls=%fused_computation.2 | custom fusion | bytes 532480 | tf_op jit(solution)/shard_map/gather | solution.py:149
  176.9 5.1 %all-to-all-start.2 = ((f32[32,16,128]{2,0,1:T(8,128)}), f32[32,16,128]{2,0,1:T(8,128)S(1)}, u32[]{:S(2)}, u32[]{:S(2)}) async-start(f32[32,16,128]{2,0,1:T(8,128)} %copy.213), calls=%async_computation.2 | async-start | bytes 524288 | tf_op jit(solution)/shard_map/all_to_all | solution.py:150
  183.9 9.7 %all-to-all-done.2 = f32[32,16,128]{2,0,1:T(8,128)S(1)} async-done(((f32[32,16,128]{2,0,1:T(8,128)}), f32[32,16,128]{2,0,1:T(8,128)S(1)}, u32[]{:S(2)}, u32[]{:S(2)}) %all-to-all-start.2) | async-done | bytes 262176 | tf_op jit(solution)/shard_map/all_to_all | solution.py:150
  194.0 9.7 %scatter_custom_fusion.3 = f32[32,256]{0,1:T(8,128)S(1)} fusion(f32[32,256]{0,1:T(8,128)S(1)} %copy.215, s32[1024]{0:T(1024)} %get-tuple-element.43, f32[1024]{0:T(1024)S(1)} %fusion.72, f32[32,2048]{0,1:T(8,128)S(1)} %bitcast.79, s32[1024]{0:T(1024)S(1)} %broadcast_clamp_fusion.1), kind=kCustom, calls=%fused_computation.131 | custom fusion | flops 65536 | bytes 1089536 | tf_op jit(solution)/shard_map/scatter-add | solution.py:156
  203.8 96.8 %all-reduce.3 = (f32[32]{0:T(128)S(1)}, f32[32]{0:T(128)S(1)}) all-reduce(f32[32]{0:T(128)S(1)} %get-tuple-element.22, f32[32]{0:T(128)S(1)} %get-tuple-element.21), channel_id=1, replica_groups=mesh['passage'=32,'sub'=16] {'passage','sub'}, use_global_device_ids=true, to_apply=%region_1.2 | all-reduce | flops 64 | bytes 512 | tf_op jit(solution)/shard_map/psum | solution.py:157
  300.6 3.8 collective-permute-start.10
  307.0 3.7 collective-permute-done.11
  312.5 94.6 %all-reduce.2 = (f32[64,64]{1,0:T(8,128)S(1)}, f32[64,64]{1,0:T(8,128)S(1)}) all-reduce(f32[64,64]{1,0:T(8,128)S(1)} %fusion.61, f32[64,64]{1,0:T(8,128)S(1)} %fusion.69), channel_id=1, replica_groups=mesh['passage'=32,'sub'=16] {'passage','sub'}, use_global_device_ids=true, to_apply=%region_11.12 | all-reduce | flops 8192 | bytes 65536 | tf_op jit(solution)/shard_map/psum | solution.py:166
  (98 shorter events, 48.8 us)
Async XLA Ops:
  0.6 182.8 %copy-start = (f32[2,4,128,128]{3,2,1,0:T(8,128)S(1)}, f32[2,4,128,128]{3,2,1,0:T(8,128)}, u32[]{:S(2)}) copy-start(f32[2,4,128,128]{3,2,1,0:T(8,128)} %param.13) | copy-start | bytes 1572868
  12.8 22.9 %all-to-all-start = ((s32[16,1,128]{2,1,0:T(1,128)}), s32[16,1,128]{2,1,0:T(1,128)S(1)}, u32[]{:S(2)}, u32[]{:S(2)}) async-start(s32[16,1,128]{2,1,0:T(1,128)} %bitcast.12), calls=%async_computation | async-start | bytes 16384 | tf_op jit(solution)/shard_map/all_to_all | solution.py:130
  35.7 18.9 %all-to-all-start.1 = ((f32[32,16,128]{2,0,1:T(8,128)}), f32[32,16,128]{2,0,1:T(8,128)S(1)}, u32[]{:S(2)}, u32[]{:S(2)}) async-start(f32[32,16,128]{2,0,1:T(8,128)} %copy.192), calls=%async_computation.1 | async-start | bytes 524288 | tf_op jit(solution)/shard_map/all_to_all | solution.py:139
  70.8 12.4 %copy-start.4 = (f32[32,256]{1,0:T(8,128)S(1)}, f32[32,256]{1,0:T(8,128)}, u32[]{:S(2)}) copy-start(f32[32,256]{1,0:T(8,128)} %param.10) | copy-start | bytes 98308
  73.9 27.9 %copy-start.1 = (f32[32,8,8,128]{3,2,1,0:T(8,128)}, f32[32,8,8,128]{3,2,1,0:T(8,128)S(1)}, u32[]{:S(2)}) copy-start(f32[32,8,8,128]{3,2,1,0:T(8,128)S(1)} %copy.195) | copy-start | bytes 3145732
  73.9 19.2 %copy-start.8 = (s32[2,4]{1,0:T(2,128)S(1)}, s32[2,4]{1,0:T(2,128)}, u32[]{:S(2)}) copy-start(s32[2,4]{1,0:T(2,128)} %param.14) | copy-start | bytes 100
  74.1 14.0 %collective-permute-start.2 = (f32[32,1,8,128]{3,2,1,0:T(8,128)S(1)}, f32[32,1,8,128]{3,2,1,0:T(8,128)S(1)}, u32[]{:S(2)}, u32[]{:S(2)}) collective-permute-start(f32[32,1,8,128]{3,2,1,0:T(8,128)S(1)} %get-tuple-element.40), channel_id=1, source_target_pairs={{0,16},{16,32},{32,48},{48,64},{64,80},{80,96},{96,112},{112,128},... | collective-permute-start | bytes 393224 | tf_op jit(solution)/shard_map/ppermute | solution.py:27
  77.2 10.9 %collective-permute-start.3 = (f32[32,1,8,128]{3,2,1,0:T(8,128)S(1)}, f32[32,1,8,128]{3,2,1,0:T(8,128)S(1)}, u32[]{:S(2)}, u32[]{:S(2)}) collective-permute-start(f32[32,1,8,128]{3,2,1,0:T(8,128)S(1)} %get-tuple-element.41), channel_id=1, source_target_pairs={{16,0},{32,16},{48,32},{64,48},{80,64},{96,80},{112,96},{128,112},... | collective-permute-start | bytes 393224 | tf_op jit(solution)/shard_map/ppermute | solution.py:30
  83.2 98.9 %collective-permute-start = (f32[32,256]{1,0:T(8,128)S(1)}, f32[32,256]{1,0:T(8,128)}, u32[]{:S(2)}, u32[]{:S(2)}) collective-permute-start(f32[32,256]{1,0:T(8,128)S(1)} %copy-done.4), channel_id=1, source_target_pairs={{0,1},{1,2},{2,3},{3,4},{4,5},{5,6},{6,7},{7,8},{8,9},{9,10},{10,1... | collective-permute-start | bytes 98312 | tf_op jit(solution)/shard_map/ppermute | solution.py:27
  85.1 97.0 %collective-permute-start.1 = (f32[32,256]{1,0:T(8,128)S(1)}, f32[32,256]{1,0:T(8,128)}, u32[]{:S(2)}, u32[]{:S(2)}) collective-permute-start(f32[32,256]{1,0:T(8,128)S(1)} %copy-done.4), channel_id=1, source_target_pairs={{1,0},{2,1},{3,2},{4,3},{5,4},{6,5},{7,6},{8,7},{9,8},{10,9},{11,1... | collective-permute-start | bytes 98312 | tf_op jit(solution)/shard_map/ppermute | solution.py:30
  88.3 6.6 %collective-permute-start.4 = (f32[32,10,1,128]{3,0,2,1:T(8,128)S(1)}, f32[32,10,1,128]{3,0,2,1:T(8,128)S(1)}, u32[]{:S(2)}, u32[]{:S(2)}) collective-permute-start(f32[32,10,1,128]{3,0,2,1:T(8,128)S(1)} %copy.231), channel_id=1, source_target_pairs={{0,1},{1,2},{2,3},{3,4},{4,5},{5,6},{6,7},{7,8},{8,9},{9,10},{10,1... | collective-permute-start | bytes 491528 | tf_op jit(solution)/shard_map/ppermute | solution.py:27
  90.9 6.7 %collective-permute-start.5 = (f32[32,10,1,128]{3,0,2,1:T(8,128)S(1)}, f32[32,10,1,128]{3,0,2,1:T(8,128)}, u32[]{:S(2)}, u32[]{:S(2)}) collective-permute-start(f32[32,10,1,128]{3,0,2,1:T(8,128)S(1)} %copy.232), channel_id=1, source_target_pairs={{1,0},{2,1},{3,2},{4,3},{5,4},{6,5},{7,6},{8,7},{9,8},{10,9},{11,1... | collective-permute-start | bytes 491528 | tf_op jit(solution)/shard_map/ppermute | solution.py:30
  107.2 31.8 %copy-start.7 = (f32[256]{0:T(256)S(1)}, f32[256]{0:T(256)}, u32[]{:S(2)}) copy-start(f32[256]{0:T(256)} %param.12) | copy-start | bytes 3076
  130.3 9.0 %collective-permute-start.6 = (f32[32,1,8,128]{3,2,1,0:T(8,128)S(1)}, f32[32,1,8,128]{3,2,1,0:T(8,128)S(1)}, u32[]{:S(2)}, u32[]{:S(2)}) collective-permute-start(f32[32,1,8,128]{3,2,1,0:T(8,128)S(1)} %get-tuple-element.38), channel_id=1, source_target_pairs={{0,16},{16,32},{32,48},{48,64},{64,80},{80,96},{96,112},{112,128},... | collective-permute-start | bytes 393224 | tf_op jit(solution)/shard_map/ppermute | solution.py:27
  132.3 8.6 %collective-permute-start.7 = (f32[32,1,8,128]{3,2,1,0:T(8,128)S(1)}, f32[32,1,8,128]{3,2,1,0:T(8,128)S(1)}, u32[]{:S(2)}, u32[]{:S(2)}) collective-permute-start(f32[32,1,8,128]{3,2,1,0:T(8,128)S(1)} %get-tuple-element.39), channel_id=1, source_target_pairs={{16,0},{32,16},{48,32},{64,48},{80,64},{96,80},{112,96},{128,112},... | collective-permute-start | bytes 393224 | tf_op jit(solution)/shard_map/ppermute | solution.py:30
  141.1 6.2 %collective-permute-start.8 = (f32[32,10,1,128]{3,0,2,1:T(8,128)S(1)}, f32[32,10,1,128]{3,0,2,1:T(8,128)S(1)}, u32[]{:S(2)}, u32[]{:S(2)}) collective-permute-start(f32[32,10,1,128]{3,0,2,1:T(8,128)S(1)} %copy.233), channel_id=1, source_target_pairs={{0,1},{1,2},{2,3},{3,4},{4,5},{5,6},{6,7},{7,8},{8,9},{9,10},{10,1... | collective-permute-start | bytes 491528 | tf_op jit(solution)/shard_map/ppermute | solution.py:27
  145.1 6.6 %collective-permute-start.9 = (f32[32,10,1,128]{3,0,2,1:T(8,128)S(1)}, f32[32,10,1,128]{3,0,2,1:T(8,128)S(1)}, u32[]{:S(2)}, u32[]{:S(2)}) collective-permute-start(f32[32,10,1,128]{3,0,2,1:T(8,128)S(1)} %copy.234), channel_id=1, source_target_pairs={{1,0},{2,1},{3,2},{4,3},{5,4},{6,5},{7,6},{8,7},{9,8},{10,9},{11,1... | collective-permute-start | bytes 491528 | tf_op jit(solution)/shard_map/ppermute | solution.py:30
  154.2 3.9 copy-start.3
  164.6 17.4 %copy-start.9 = (s32[8]{0:T(128)S(1)}, s32[8]{0:T(128)}, u32[]{:S(2)}) copy-start(s32[8]{0:T(128)} %reshape.107) | copy-start | bytes 100
  168.2 35.5 %copy-start.6 = (f32[256]{0:T(256)S(1)}, f32[256]{0:T(256)}, u32[]{:S(2)}) copy-start(f32[256]{0:T(256)} %param.11) | copy-start | bytes 3076
  176.9 16.8 %all-to-all-start.2 = ((f32[32,16,128]{2,0,1:T(8,128)}), f32[32,16,128]{2,0,1:T(8,128)S(1)}, u32[]{:S(2)}, u32[]{:S(2)}) async-start(f32[32,16,128]{2,0,1:T(8,128)} %copy.213), calls=%async_computation.2 | async-start | bytes 524288 | tf_op jit(solution)/shard_map/all_to_all | solution.py:150
  300.6 6.3 %collective-permute-start.10 = (f32[32,256]{0,1:T(8,128)S(1)}, f32[32,256]{0,1:T(8,128)S(1)}, u32[]{:S(2)}, u32[]{:S(2)}) collective-permute-start(f32[32,256]{0,1:T(8,128)S(1)} %multiply_subtract_fusion), channel_id=1, source_target_pairs={{0,1},{1,2},{2,3},{3,4},{4,5},{5,6},{6,7},{7,8},{8,9},{9,10},{10,1... | collective-permute-start | bytes 98312 | tf_op jit(solution)/shard_map/ppermute | solution.py:27
  304.5 6.3 %collective-permute-start.11 = (f32[32,256]{0,1:T(8,128)S(1)}, f32[32,256]{0,1:T(8,128)S(1)}, u32[]{:S(2)}, u32[]{:S(2)}) collective-permute-start(f32[32,256]{0,1:T(8,128)S(1)} %multiply_subtract_fusion), channel_id=1, source_target_pairs={{1,0},{2,1},{3,2},{4,3},{5,4},{6,5},{7,6},{8,7},{9,8},{10,9},{11,1... | collective-permute-start | bytes 98312 | tf_op jit(solution)/shard_map/ppermute | solution.py:30
  306.9 100.7 %copy-start.5 = (f32[32,256]{1,0:T(8,128)}, f32[32,256]{1,0:T(8,128)S(1)}, u32[]{:S(2)}) copy-start(f32[32,256]{1,0:T(8,128)S(1)} %copy.224) | copy-start | bytes 98308
  (1 other events, 3.9 us)
where the time goes:
time: 409 us; the launch traced here: 408 us
  blocking collectives  191 us (47%)
  other arithmetic  87.8 us (21%)
  starting transfers between devices  63 us (15%)
  waiting for transfers between devices  34.2 us (8%)
  local copies, waits for them, and re-layouts  27.8 us (7%)
    psum x1, blocking collectives, body(): lax.psum((jnp.sum(block_vectors * stiff_image, axis=1), jnp.sum(block_vec...  96.8 us
    psum x1, blocking collectives, body(): lax.psum((inner(search, image), inner(search, search)), ('passage', 'sub'))  94.6 us
    add x1, other arithmetic, pressure_solve(): second = first + second_step  23.2 us
    ppermute x6, starting transfers between devices, padded_2(): lax.ppermute(lax.slice_in_dim(block, 0, width, axis=dim), axis, backward)  21.6 us
    ppermute x6, starting transfers between devices, padded_2(): lax.ppermute(lax.slice_in_dim(block, block.shape[dim] - width, None, axis...  17.4 us
    scatter-add x1, other arithmetic, body(): source = jnp.zeros((modes, CX * CY * CZ), jnp.float32).at[:, cells_in].ad...  15.8 us
    concatenate x4, other arithmetic, padded_2(): block = jnp.concatenate([low, block, high], axis=dim)  14.5 us
    ppermute x6, waiting for transfers between devices, padded_2(): lax.ppermute(lax.slice_in_dim(block, 0, width, axis=dim), axis, backward)  12.1 us
  transfers between devices with their start and end apart: 15, of which 8 were waited for; matrix products, arithmetic and copies ran while one was open for 18% of the time, Pallas kernels for 0%

commit v1 on v0

--- a/solution.py
+++ b/solution.py
@@ -164,7 +164,7 @@
     search = jnp.concatenate([block_vectors, residual], axis=0)
     image = jnp.concatenate([stiff_image, stiff_resid], axis=0)
     gram_stiff, gram_plain = lax.psum(
-        (inner(search, image), inner(search, search)), ("passage", "sub")
+        lax.psum((inner(search, image), inner(search, search)), "passage"), "sub"
     )
     return (residual, gram_stiff / total, gram_plain / total)
 

time: 409 us -> 494 us (1.21)
  blocking collectives: 191 us -> 275 us
    psum x1 -> x2, blocking collectives: 94.6 us -> 178 us  [the longest x1 111 us: body(): lax.psum((inner(search, image), inner(search, search)), 'passage')]
  transfers between devices with their start and end apart: 15 -> 15, of which waited for: 8 -> 8; matrix products, arithmetic and copies ran while one was open for 18% -> 15% of each run, Pallas kernels for 0% -> 0%
where the time goes in v1:
time: 494 us; the launch traced here: 493 us
  blocking collectives  275 us (56%)
  other arithmetic  88.7 us (18%)
  starting transfers between devices  63 us (13%)
  waiting for transfers between devices  34.2 us (7%)
  local copies, waits for them, and re-layouts  27.8 us (6%)
    psum x1, blocking collectives, body(): lax.psum((inner(search, image), inner(search, search)), 'passage')  111 us
    psum x1, blocking collectives, body(): lax.psum((jnp.sum(block_vectors * stiff_image, axis=1), jnp.sum(block_vec...  96.8 us
    psum x1, blocking collectives, body(): lax.psum(lax.psum((inner(search, image), inner(search, search)), 'passage...  67.9 us
    add x1, other arithmetic, pressure_solve(): second = first + second_step  24 us
    ppermute x6, starting transfers between devices, padded_2(): lax.ppermute(lax.slice_in_dim(block, 0, width, axis=dim), axis, backward)  21.6 us
    ppermute x6, starting transfers between devices, padded_2(): lax.ppermute(lax.slice_in_dim(block, block.shape[dim] - width, None, axis...  17.4 us
    scatter-add x1, other arithmetic, body(): source = jnp.zeros((modes, CX * CY * CZ), jnp.float32).at[:, cells_in].ad...  15.8 us
    concatenate x4, other arithmetic, padded_2(): block = jnp.concatenate([low, block, high], axis=dim)  14.5 us
  transfers between devices with their start and end apart: 15, of which 8 were waited for; matrix products, arithmetic and copies ran while one was open for 15% of the time, Pallas kernels for 0%

profile of v1, /device:TPU:1, one launch (start us, length us, event | category | flops | bytes accessed | tf_op | source)
XLA Modules:
  0.0 492.6 jit_solution(8689169876800533)
XLA Ops:
  1.4 4.5 reduce-window.6
  7.7 5.0 %scatter_custom_fusion = s32[2048]{0:T(1024)} fusion(s32[1024]{0:T(1024)S(1)} %bitcast.91, s32[1024]{0:T(1024)} %param.17, s32[]{:T(128)} %constant.17.clone.1), kind=kCustom, calls=%fused_computation.178 | custom fusion | bytes 8704 | tf_op jit(solution)/shard_map/scatter | solution.py:127
  12.8 11.8 %all-to-all-start = ((s32[16,1,128]{2,1,0:T(1,128)}), s32[16,1,128]{2,1,0:T(1,128)S(1)}, u32[]{:S(2)}, u32[]{:S(2)}) async-start(s32[16,1,128]{2,1,0:T(1,128)} %bitcast.12), calls=%async_computation | async-start | bytes 16384 | tf_op jit(solution)/shard_map/all_to_all | solution.py:130
  28.1 6.6 %scatter_custom_fusion.1 = f32[32,2048]{0,1:T(8,128)S(1)} fusion(s32[1024]{0:T(1024)S(1)} %bitcast.92, f32[]{:T(128)} %constant.19.clone.1, f32[1024]{0:T(1024)S(1)} %fusion.72, f32[32,256]{0,1:T(8,128)S(1)} %copy.184, s32[1024]{0:T(1024)S(1)} %get-tuple-element.44), kind=kCustom, calls=%fused_computation.133 | custom fusion | flops 32768 | bytes 401412 | tf_op jit(solution)/shard_map/scatter | solution.py:136
  35.7 7.2 %all-to-all-start.1 = ((f32[32,16,128]{2,0,1:T(8,128)}), f32[32,16,128]{2,0,1:T(8,128)S(1)}, u32[]{:S(2)}, u32[]{:S(2)}) async-start(f32[32,16,128]{2,0,1:T(8,128)} %copy.192), calls=%async_computation.1 | async-start | bytes 524288 | tf_op jit(solution)/shard_map/all_to_all | solution.py:139
  42.9 11.7 %all-to-all-done.1 = f32[32,16,128]{2,0,1:T(8,128)S(1)} async-done(((f32[32,16,128]{2,0,1:T(8,128)}), f32[32,16,128]{2,0,1:T(8,128)S(1)}, u32[]{:S(2)}, u32[]{:S(2)}) %all-to-all-start.1) | async-done | bytes 262176 | tf_op jit(solution)/shard_map/all_to_all | solution.py:139
  55.0 15.8 %scatter_custom_fusion.2 = f32[32,8192]{0,1:T(8,128)} fusion(s32[2048]{0:T(1024)S(1)} %bitcast.87, f32[2048,32]{1,0:T(8,128)S(1)} %copy.194, f32[]{:T(128)} %constant.19.clone.1), kind=kCustom, calls=%fused_computation.24 | custom fusion | flops 65536 | bytes 1048580 | tf_op jit(solution)/shard_map/scatter-add | solution.py:145
  77.2 6.0 %collective-permute-start.3 = (f32[32,1,8,128]{3,2,1,0:T(8,128)S(1)}, f32[32,1,8,128]{3,2,1,0:T(8,128)S(1)}, u32[]{:S(2)}, u32[]{:S(2)}) collective-permute-start(f32[32,1,8,128]{3,2,1,0:T(8,128)S(1)} %get-tuple-element.43), channel_id=1, source_target_pairs={{16,0},{32,16},{48,32},{64,48},{80,64},{96,80},{112,96},{128,112},... | collective-permute-start | bytes 393224 | tf_op jit(solution)/shard_map/ppermute | solution.py:30
  101.8 5.4 %select_maximum_fusion.4 = f32[32,10,10,130]{3,2,1,0:T(8,128)} fusion(f32[32,10,1,128]{3,2,1,0:T(1,128)S(1)} %copy.201, f32[32,10,1,128]{3,2,1,0:T(1,128)S(1)} %copy.200, f32[32,1,8,128]{3,2,1,0:T(8,128)S(1)} %collective-permute-done.3, f32[32,8,8,128]{3,2,1,0:T(8,128)S(1)} %broadcast_multiply_fusion, f32[32,1,8,128]{3,2,1,0:T(8,128)S(1)} %collective-permute-done.2), kind=kLoop, calls=%fused_computation.15 | loop fusion | flops 4992000 | bytes 3302400 | tf_op jit(solution)/shard_map/concatenate | solution.py:31
  107.2 24.0 %fusion.77 = (f32[32,8,8,128]{3,2,1,0:T(8,128)S(1)}, f32[32,8,8,128]{3,2,1,0:T(8,128)}) fusion(f32[32,8,8,128]{3,2,1,0:T(8,128)} %copy-done.1, f32[32,10,10,130]{3,2,1,0:T(8,128)} %select_maximum_fusion.4, f32[32,10,9,128]{3,2,1,0:T(8,128)} %get-tuple-element.37, f32[32,1,8,128]{3,2,1,0:T(8,128)S(1)} %collective-permute-done.3, ...), kind=kLoop, calls=%fused_computation.188 | loop fusion | flops 14417920 | bytes 29622272 | tf_op jit(solution)/shard_map/add | solution.py:72
  133.1 6.7 %collective-permute-start.7 = (f32[32,1,8,128]{3,2,1,0:T(8,128)S(1)}, f32[32,1,8,128]{3,2,1,0:T(8,128)S(1)}, u32[]{:S(2)}, u32[]{:S(2)}) collective-permute-start(f32[32,1,8,128]{3,2,1,0:T(8,128)S(1)} %get-tuple-element.41), channel_id=1, source_target_pairs={{16,0},{32,16},{48,32},{64,48},{80,64},{96,80},{112,96},{128,112},... | collective-permute-start | bytes 393224 | tf_op jit(solution)/shard_map/ppermute | solution.py:30
  142.0 4.0 collective-permute-start.8
  148.4 4.2 collective-permute-done.9
  155.0 3.9 select_maximum_fusion
  158.9 6.6 %fusion.8 = f32[32,8,8,128]{3,2,1,0:T(8,128)} fusion(f32[32,8,8,128]{3,2,1,0:T(8,128)S(1)} %get-tuple-element.30, f32[32,8,8,128]{3,2,1,0:T(8,128)S(1)} %copy-done.2, f32[32,10,10,130]{3,2,1,0:T(8,128)S(1)} %select_maximum_fusion, f32[32,10,9,128]{3,2,1,0:T(8,128)} %get-tuple-element.33, f32[32,1,8,128]{3,2,1,0:T(8,128)S(1)} %collective-permute-done.7, ...), kind=kLoop, calls=%fused_computation.34 | loop fusion | flops 14155776 | bytes 29622272 | tf_op jit(solution)/shard_map/add | solution.py:77
  169.2 7.7 %gather_fusion.1 = f32[2048,32]{1,0:T(8,128)S(1)} fusion(f32[32,8192]{0,1:T(8,128)} %bitcast.78, s32[2048]{0:T(1024)S(1)} %broadcast_clamp_fusion), kind=kCustom, calls=%fused_computation.2 | custom fusion | bytes 532480 | tf_op jit(solution)/shard_map/gather | solution.py:149
  177.8 5.1 %all-to-all-start.2 = ((f32[32,16,128]{2,0,1:T(8,128)}), f32[32,16,128]{2,0,1:T(8,128)S(1)}, u32[]{:S(2)}, u32[]{:S(2)}) async-start(f32[32,16,128]{2,0,1:T(8,128)} %copy.213), calls=%async_computation.2 | async-start | bytes 524288 | tf_op jit(solution)/shard_map/all_to_all | solution.py:150
  184.9 9.7 %all-to-all-done.2 = f32[32,16,128]{2,0,1:T(8,128)S(1)} async-done(((f32[32,16,128]{2,0,1:T(8,128)}), f32[32,16,128]{2,0,1:T(8,128)S(1)}, u32[]{:S(2)}, u32[]{:S(2)}) %all-to-all-start.2) | async-done | bytes 262176 | tf_op jit(solution)/shard_map/all_to_all | solution.py:150
  195.0 9.7 %scatter_custom_fusion.3 = f32[32,256]{0,1:T(8,128)S(1)} fusion(f32[32,256]{0,1:T(8,128)S(1)} %copy.215, s32[1024]{0:T(1024)} %get-tuple-element.45, f32[1024]{0:T(1024)S(1)} %fusion.72, f32[32,2048]{0,1:T(8,128)S(1)} %bitcast.79, s32[1024]{0:T(1024)S(1)} %broadcast_clamp_fusion.1), kind=kCustom, calls=%fused_computation.131 | custom fusion | flops 65536 | bytes 1089536 | tf_op jit(solution)/shard_map/scatter-add | solution.py:156
  204.8 96.8 %all-reduce.2 = (f32[32]{0:T(128)S(1)}, f32[32]{0:T(128)S(1)}) all-reduce(f32[32]{0:T(128)S(1)} %get-tuple-element.22, f32[32]{0:T(128)S(1)} %get-tuple-element.21), channel_id=1, replica_groups=mesh['passage'=32,'sub'=16] {'passage','sub'}, use_global_device_ids=true, to_apply=%region_1.2 | all-reduce | flops 64 | bytes 512 | tf_op jit(solution)/shard_map/psum | solution.py:157
  301.6 3.8 collective-permute-start.10
  308.0 3.7 collective-permute-done.11
  313.5 110.6 %all-reduce.3 = (f32[64,64]{1,0:T(8,128)S(1)}, f32[64,64]{1,0:T(8,128)S(1)}) all-reduce(f32[64,64]{1,0:T(8,128)S(1)} %fusion.61, f32[64,64]{1,0:T(8,128)S(1)} %fusion.69), channel_id=1, replica_groups=mesh['passage'=32,'sub'=16] {'passage'}, use_global_device_ids=true, to_apply=%region_11.12 | all-reduce | flops 8192 | bytes 65536 | tf_op jit(solution)/shard_map/psum | solution.py:167
  424.1 67.9 %all-reduce.4 = (f32[64,64]{1,0:T(8,128)S(1)}, f32[64,64]{1,0:T(8,128)S(1)}) all-reduce(f32[64,64]{1,0:T(8,128)S(1)} %get-tuple-element.25, f32[64,64]{1,0:T(8,128)S(1)} %get-tuple-element.26), channel_id=1, replica_groups=mesh['passage'=32,'sub'=16] {'sub'}, use_global_device_ids=true, to_apply=%region_12.13 | all-reduce | flops 8192 | bytes 65536 | tf_op jit(solution)/shard_map/psum | solution.py:166
  (99 shorter events, 52.5 us)
Async XLA Ops:
  0.6 183.8 %copy-start = (f32[2,4,128,128]{3,2,1,0:T(8,128)S(1)}, f32[2,4,128,128]{3,2,1,0:T(8,128)}, u32[]{:S(2)}) copy-start(f32[2,4,128,128]{3,2,1,0:T(8,128)} %param.13) | copy-start | bytes 1572868
  12.8 22.9 %all-to-all-start = ((s32[16,1,128]{2,1,0:T(1,128)}), s32[16,1,128]{2,1,0:T(1,128)S(1)}, u32[]{:S(2)}, u32[]{:S(2)}) async-start(s32[16,1,128]{2,1,0:T(1,128)} %bitcast.12), calls=%async_computation | async-start | bytes 16384 | tf_op jit(solution)/shard_map/all_to_all | solution.py:130
  35.7 18.9 %all-to-all-start.1 = ((f32[32,16,128]{2,0,1:T(8,128)}), f32[32,16,128]{2,0,1:T(8,128)S(1)}, u32[]{:S(2)}, u32[]{:S(2)}) async-start(f32[32,16,128]{2,0,1:T(8,128)} %copy.192), calls=%async_computation.1 | async-start | bytes 524288 | tf_op jit(solution)/shard_map/all_to_all | solution.py:139
  70.8 12.4 %copy-start.4 = (f32[32,256]{1,0:T(8,128)S(1)}, f32[32,256]{1,0:T(8,128)}, u32[]{:S(2)}) copy-start(f32[32,256]{1,0:T(8,128)} %param.10) | copy-start | bytes 98308
  73.9 28.0 %copy-start.1 = (f32[32,8,8,128]{3,2,1,0:T(8,128)}, f32[32,8,8,128]{3,2,1,0:T(8,128)S(1)}, u32[]{:S(2)}) copy-start(f32[32,8,8,128]{3,2,1,0:T(8,128)S(1)} %copy.195) | copy-start | bytes 3145732
  73.9 19.2 %copy-start.8 = (s32[2,4]{1,0:T(2,128)S(1)}, s32[2,4]{1,0:T(2,128)}, u32[]{:S(2)}) copy-start(s32[2,4]{1,0:T(2,128)} %param.14) | copy-start | bytes 100
  74.1 14.0 %collective-permute-start.2 = (f32[32,1,8,128]{3,2,1,0:T(8,128)S(1)}, f32[32,1,8,128]{3,2,1,0:T(8,128)S(1)}, u32[]{:S(2)}, u32[]{:S(2)}) collective-permute-start(f32[32,1,8,128]{3,2,1,0:T(8,128)S(1)} %get-tuple-element.42), channel_id=1, source_target_pairs={{0,16},{16,32},{32,48},{48,64},{64,80},{80,96},{96,112},{112,128},... | collective-permute-start | bytes 393224 | tf_op jit(solution)/shard_map/ppermute | solution.py:27
  77.2 10.9 %collective-permute-start.3 = (f32[32,1,8,128]{3,2,1,0:T(8,128)S(1)}, f32[32,1,8,128]{3,2,1,0:T(8,128)S(1)}, u32[]{:S(2)}, u32[]{:S(2)}) collective-permute-start(f32[32,1,8,128]{3,2,1,0:T(8,128)S(1)} %get-tuple-element.43), channel_id=1, source_target_pairs={{16,0},{32,16},{48,32},{64,48},{80,64},{96,80},{112,96},{128,112},... | collective-permute-start | bytes 393224 | tf_op jit(solution)/shard_map/ppermute | solution.py:30
  83.2 99.9 %collective-permute-start = (f32[32,256]{1,0:T(8,128)S(1)}, f32[32,256]{1,0:T(8,128)}, u32[]{:S(2)}, u32[]{:S(2)}) collective-permute-start(f32[32,256]{1,0:T(8,128)S(1)} %copy-done.4), channel_id=1, source_target_pairs={{0,1},{1,2},{2,3},{3,4},{4,5},{5,6},{6,7},{7,8},{8,9},{9,10},{10,1... | collective-permute-start | bytes 98312 | tf_op jit(solution)/shard_map/ppermute | solution.py:27
  85.1 98.0 %collective-permute-start.1 = (f32[32,256]{1,0:T(8,128)S(1)}, f32[32,256]{1,0:T(8,128)}, u32[]{:S(2)}, u32[]{:S(2)}) collective-permute-start(f32[32,256]{1,0:T(8,128)S(1)} %copy-done.4), channel_id=1, source_target_pairs={{1,0},{2,1},{3,2},{4,3},{5,4},{6,5},{7,6},{8,7},{9,8},{10,9},{11,1... | collective-permute-start | bytes 98312 | tf_op jit(solution)/shard_map/ppermute | solution.py:30
  88.3 6.6 %collective-permute-start.4 = (f32[32,10,1,128]{3,0,2,1:T(8,128)S(1)}, f32[32,10,1,128]{3,0,2,1:T(8,128)S(1)}, u32[]{:S(2)}, u32[]{:S(2)}) collective-permute-start(f32[32,10,1,128]{3,0,2,1:T(8,128)S(1)} %copy.231), channel_id=1, source_target_pairs={{0,1},{1,2},{2,3},{3,4},{4,5},{5,6},{6,7},{7,8},{8,9},{9,10},{10,1... | collective-permute-start | bytes 491528 | tf_op jit(solution)/shard_map/ppermute | solution.py:27
  90.9 6.7 %collective-permute-start.5 = (f32[32,10,1,128]{3,0,2,1:T(8,128)S(1)}, f32[32,10,1,128]{3,0,2,1:T(8,128)}, u32[]{:S(2)}, u32[]{:S(2)}) collective-permute-start(f32[32,10,1,128]{3,0,2,1:T(8,128)S(1)} %copy.232), channel_id=1, source_target_pairs={{1,0},{2,1},{3,2},{4,3},{5,4},{6,5},{7,6},{8,7},{9,8},{10,9},{11,1... | collective-permute-start | bytes 491528 | tf_op jit(solution)/shard_map/ppermute | solution.py:30
  107.2 32.6 %copy-start.7 = (f32[256]{0:T(256)S(1)}, f32[256]{0:T(256)}, u32[]{:S(2)}) copy-start(f32[256]{0:T(256)} %param.12) | copy-start | bytes 3076
  131.2 9.0 %collective-permute-start.6 = (f32[32,1,8,128]{3,2,1,0:T(8,128)S(1)}, f32[32,1,8,128]{3,2,1,0:T(8,128)S(1)}, u32[]{:S(2)}, u32[]{:S(2)}) collective-permute-start(f32[32,1,8,128]{3,2,1,0:T(8,128)S(1)} %get-tuple-element.40), channel_id=1, source_target_pairs={{0,16},{16,32},{32,48},{48,64},{64,80},{80,96},{96,112},{112,128},... | collective-permute-start | bytes 393224 | tf_op jit(solution)/shard_map/ppermute | solution.py:27
  133.1 8.6 %collective-permute-start.7 = (f32[32,1,8,128]{3,2,1,0:T(8,128)S(1)}, f32[32,1,8,128]{3,2,1,0:T(8,128)S(1)}, u32[]{:S(2)}, u32[]{:S(2)}) collective-permute-start(f32[32,1,8,128]{3,2,1,0:T(8,128)S(1)} %get-tuple-element.41), channel_id=1, source_target_pairs={{16,0},{32,16},{48,32},{64,48},{80,64},{96,80},{112,96},{128,112},... | collective-permute-start | bytes 393224 | tf_op jit(solution)/shard_map/ppermute | solution.py:30
  142.0 6.2 %collective-permute-start.8 = (f32[32,10,1,128]{3,0,2,1:T(8,128)S(1)}, f32[32,10,1,128]{3,0,2,1:T(8,128)S(1)}, u32[]{:S(2)}, u32[]{:S(2)}) collective-permute-start(f32[32,10,1,128]{3,0,2,1:T(8,128)S(1)} %copy.233), channel_id=1, source_target_pairs={{0,1},{1,2},{2,3},{3,4},{4,5},{5,6},{6,7},{7,8},{8,9},{9,10},{10,1... | collective-permute-start | bytes 491528 | tf_op jit(solution)/shard_map/ppermute | solution.py:27
  146.0 6.6 %collective-permute-start.9 = (f32[32,10,1,128]{3,0,2,1:T(8,128)S(1)}, f32[32,10,1,128]{3,0,2,1:T(8,128)S(1)}, u32[]{:S(2)}, u32[]{:S(2)}) collective-permute-start(f32[32,10,1,128]{3,0,2,1:T(8,128)S(1)} %copy.234), channel_id=1, source_target_pairs={{1,0},{2,1},{3,2},{4,3},{5,4},{6,5},{7,6},{8,7},{9,8},{10,9},{11,1... | collective-permute-start | bytes 491528 | tf_op jit(solution)/shard_map/ppermute | solution.py:30
  155.0 3.9 copy-start.3
  165.5 17.4 %copy-start.9 = (s32[8]{0:T(128)S(1)}, s32[8]{0:T(128)}, u32[]{:S(2)}) copy-start(s32[8]{0:T(128)} %reshape.107) | copy-start | bytes 100
  169.2 35.5 %copy-start.6 = (f32[256]{0:T(256)S(1)}, f32[256]{0:T(256)}, u32[]{:S(2)}) copy-start(f32[256]{0:T(256)} %param.11) | copy-start | bytes 3076
  177.8 16.8 %all-to-all-start.2 = ((f32[32,16,128]{2,0,1:T(8,128)}), f32[32,16,128]{2,0,1:T(8,128)S(1)}, u32[]{:S(2)}, u32[]{:S(2)}) async-start(f32[32,16,128]{2,0,1:T(8,128)} %copy.213), calls=%async_computation.2 | async-start | bytes 524288 | tf_op jit(solution)/shard_map/all_to_all | solution.py:150
  301.6 6.3 %collective-permute-start.10 = (f32[32,256]{0,1:T(8,128)S(1)}, f32[32,256]{0,1:T(8,128)S(1)}, u32[]{:S(2)}, u32[]{:S(2)}) collective-permute-start(f32[32,256]{0,1:T(8,128)S(1)} %multiply_subtract_fusion), channel_id=1, source_target_pairs={{0,1},{1,2},{2,3},{3,4},{4,5},{5,6},{6,7},{7,8},{8,9},{9,10},{10,1... | collective-permute-start | bytes 98312 | tf_op jit(solution)/shard_map/ppermute | solution.py:27
  305.4 6.3 %collective-permute-start.11 = (f32[32,256]{0,1:T(8,128)S(1)}, f32[32,256]{0,1:T(8,128)S(1)}, u32[]{:S(2)}, u32[]{:S(2)}) collective-permute-start(f32[32,256]{0,1:T(8,128)S(1)} %multiply_subtract_fusion), channel_id=1, source_target_pairs={{1,0},{2,1},{3,2},{4,3},{5,4},{6,5},{7,6},{8,7},{9,8},{10,9},{11,1... | collective-permute-start | bytes 98312 | tf_op jit(solution)/shard_map/ppermute | solution.py:30
  307.9 184.7 %copy-start.5 = (f32[32,256]{1,0:T(8,128)}, f32[32,256]{1,0:T(8,128)S(1)}, u32[]{:S(2)}) copy-start(f32[32,256]{1,0:T(8,128)S(1)} %copy.224) | copy-start | bytes 98308
  (1 other events, 3.9 us)
